TPU v7x, 256 devices: a whole 4x4x8 slice. The times are simulated.
256 devices in a mesh: ctx: 16 (over y, x_lo, core), head: 16 (over x_hi, z).
Axes of the slice: x: 4 (x_hi: 2, x_lo: 2; x = x_hi * 2 + x_lo), y: 4, z: 8, core: 2. Of those that a mesh axis runs over, the one named last changes fastest.
Arguments:
- inputs: bfloat16 [8192, 2048], P('ctx'), may hold values from -6 to 6
- tangents: bfloat16 [8192, 2048], P('ctx'), may hold values from -6 to 6
- w_qkv: bfloat16 [3, 2048, 2048], P(None, None, 'head'), may hold values from -0.125 to 0.125
- w_out: bfloat16 [2048, 2048], P('head'), may hold values from -0.1875 to 0.1875
Outputs:
- attended: bfloat16 [8192, 2048], P('ctx', 'head')
- attended_tangent: bfloat16 [8192, 2048], P('ctx', 'head')
All inputs are finite; a program needn't handle non-finite values.
Results may differ from a plain program's by a relative error of at most 0.023.
Values may be sent and summed in bfloat16 or wider, within the bound.
A program may use at most 64 MiB of HBM per device.

v0:
```python
import jax
import jax.numpy as jnp
from jax import lax
from jax.sharding import PartitionSpec as P

HD = 128


def shifted(value, axis, steps):
    count = lax.axis_size(axis)
    pairs = [(source, (source + steps) % count) for source in range(count)]
    return lax.ppermute(value, axis, pairs)


def local(inputs, tangents, w_qkv, w_out):
    tok_rows = inputs.shape[0]
    local_heads = w_qkv.shape[2] // HD
    scale = HD ** (-0.5)

    def project(rows, index):
        flat = jnp.dot(rows, w_qkv[index], preferred_element_type=jnp.float32).astype(jnp.bfloat16)
        return flat.reshape(tok_rows, local_heads, HD)

    queries = project(inputs, 0)
    tqueries = project(tangents, 0)
    own_block = jnp.stack(
        [project(inputs, 1), project(inputs, 2), project(tangents, 1), project(tangents, 2)]
    )

    def absorb(state, carried):
        top, total, spread, accum, taccum = state
        keys, values, tkeys, tvalues = (carried[0], carried[1], carried[2], carried[3])
        scores = (
            jnp.einsum("qhd,khd->qhk", queries, keys, preferred_element_type=jnp.float32) * scale
        )
        tscores = (
            jnp.einsum("qhd,khd->qhk", tqueries, keys, preferred_element_type=jnp.float32)
            + jnp.einsum("qhd,khd->qhk", queries, tkeys, preferred_element_type=jnp.float32)
        ) * scale
        new_top = jnp.maximum(top, jnp.max(scores, axis=2))
        factor = jnp.exp(top - new_top)
        weights = jnp.exp(scores - new_top[:, :, None])
        mixed = weights * tscores
        total = factor * total + jnp.sum(weights, axis=2)
        spread = factor * spread + jnp.sum(mixed, axis=2)
        weights_b = weights.astype(jnp.bfloat16)
        mixed_b = mixed.astype(jnp.bfloat16)
        accum = factor[:, :, None] * accum + jnp.einsum(
            "qhk,khd->qhd", weights_b, values, preferred_element_type=jnp.float32
        )
        taccum = (
            factor[:, :, None] * taccum
            + jnp.einsum("qhk,khd->qhd", mixed_b, values, preferred_element_type=jnp.float32)
            + jnp.einsum("qhk,khd->qhd", weights_b, tvalues, preferred_element_type=jnp.float32)
        )
        return (new_top, total, spread, accum, taccum)

    zeros_row = jnp.zeros((tok_rows, local_heads), jnp.float32)
    zeros_acc = jnp.zeros((tok_rows, local_heads, HD), jnp.float32)
    start_state = (
        jnp.full((tok_rows, local_heads), -jnp.inf, jnp.float32),
        zeros_row,
        zeros_row,
        zeros_acc,
        zeros_acc,
    )
    state = absorb(start_state, own_block)
    cycle_size = lax.axis_size("ctx")

    def step_one(index, carry):
        carried, inner = carry
        carried = shifted(carried, "ctx", 1)
        return (carried, absorb(inner, carried))

    carried, state = lax.fori_loop(0, cycle_size - 1, step_one, (own_block, state))
    top, total, spread, accum, taccum = state
    heads_out = accum / total[:, :, None]
    heads_tangent = taccum / total[:, :, None] - (spread / total)[:, :, None] * heads_out
    heads_out = heads_out.astype(jnp.bfloat16).reshape(tok_rows, local_heads * HD)
    heads_tangent = heads_tangent.astype(jnp.bfloat16).reshape(tok_rows, local_heads * HD)
    stacked = jnp.stack([heads_out, heads_tangent])
    partial_terms = jnp.einsum("sqc,cd->sqd", stacked, w_out, preferred_element_type=jnp.float32)
    summed = lax.psum_scatter(partial_terms, "head", scatter_dimension=2, tiled=True)
    return (summed[0].astype(jnp.bfloat16), summed[1].astype(jnp.bfloat16))


def solution(mesh):
    return jax.shard_map(
        local,
        mesh=mesh,
        in_specs=(P("ctx", None), P("ctx", None), P(None, None, "head"), P("head", None)),
        out_specs=(P("ctx", "head"), P("ctx", "head")),
        check_vma=False,
    )
```

profile of v0, /device:TPU:8, one launch (start us, length us, event | category | flops | bytes accessed | tf_op | source)
XLA Modules:
  0.0 476.8 jit_solution(654049857911514875)
XLA Ops:
  7.2 1.5 copy-done
  8.8 1.9 convolution_convert_fusion.5
  10.6 0.7 convolution_convert_fusion.1
  11.4 0.7 convolution_convert_fusion.4
  12.1 0.9 copy-done.2
  13.0 0.7 convolution_convert_fusion.3
  13.7 0.7 convolution_convert_fusion
  14.4 0.7 convolution_convert_fusion.2
  16.3 1.0 fusion.58
  17.6 1.0 fusion.25
  18.6 1.1 copy.12
  19.8 0.7 fusion.53
  20.5 1.8 pad_maximum_fusion
  22.2 195.3 %while.20 = (s32[]{:T(128)}, bf16[4,512,1,128]{3,1,2,0:T(8,128)(2,1)}, f32[512,1]{0,1:T(1,128)S(1)}, f32[512,1]{0,1:T(1,128)S(1)}, f32[512,1]{0,1:T(1,128)S(1)},...) while((s32[]{:T(128)}, ...), condition=%wide.region_7.0_spmd, body=%wide.region_3.0_spmd.sunk | while | flops 406652416 | bytes 14336141 | solution.py:75
  22.2 9.7 %collective-permute-done = bf16[4,512,1,128]{3,1,2,0:T(8,128)(2,1)S(1)} collective-permute-done((bf16[4,512,1,128]{3,1,2,0:T(8,128)(2,1)}, bf16[4,512,1,128]{3,1,2,0:T(8,128)(2,1)S(1)}, u32[]{:S(2)}, u32[]{:S(2)}) %collective-permute-start) | collective-permute-done | bytes 524320 | tf_op jit(solution)/shard_map/while/body/eval_jaxpr/ppermute | solution.py:12
  33.2 0.8 copy.28
  35.3 9.7 %collective-permute-done = bf16[4,512,1,128]{3,1,2,0:T(8,128)(2,1)S(1)} collective-permute-done((bf16[4,512,1,128]{3,1,2,0:T(8,128)(2,1)}, bf16[4,512,1,128]{3,1,2,0:T(8,128)(2,1)S(1)}, u32[]{:S(2)}, u32[]{:S(2)}) %collective-permute-start) | collective-permute-done | bytes 524320 | tf_op jit(solution)/shard_map/while/body/eval_jaxpr/ppermute | solution.py:12
  46.3 0.8 copy.28
  48.3 9.7 %collective-permute-done = bf16[4,512,1,128]{3,1,2,0:T(8,128)(2,1)S(1)} collective-permute-done((bf16[4,512,1,128]{3,1,2,0:T(8,128)(2,1)}, bf16[4,512,1,128]{3,1,2,0:T(8,128)(2,1)S(1)}, u32[]{:S(2)}, u32[]{:S(2)}) %collective-permute-start) | collective-permute-done | bytes 524320 | tf_op jit(solution)/shard_map/while/body/eval_jaxpr/ppermute | solution.py:12
  59.3 0.8 copy.28
  61.3 9.7 %collective-permute-done = bf16[4,512,1,128]{3,1,2,0:T(8,128)(2,1)S(1)} collective-permute-done((bf16[4,512,1,128]{3,1,2,0:T(8,128)(2,1)}, bf16[4,512,1,128]{3,1,2,0:T(8,128)(2,1)S(1)}, u32[]{:S(2)}, u32[]{:S(2)}) %collective-permute-start) | collective-permute-done | bytes 524320 | tf_op jit(solution)/shard_map/while/body/eval_jaxpr/ppermute | solution.py:12
  72.3 0.8 copy.28
  74.3 9.7 %collective-permute-done = bf16[4,512,1,128]{3,1,2,0:T(8,128)(2,1)S(1)} collective-permute-done((bf16[4,512,1,128]{3,1,2,0:T(8,128)(2,1)}, bf16[4,512,1,128]{3,1,2,0:T(8,128)(2,1)S(1)}, u32[]{:S(2)}, u32[]{:S(2)}) %collective-permute-start) | collective-permute-done | bytes 524320 | tf_op jit(solution)/shard_map/while/body/eval_jaxpr/ppermute | solution.py:12
  85.3 0.8 copy.28
  87.4 9.7 %collective-permute-done = bf16[4,512,1,128]{3,1,2,0:T(8,128)(2,1)S(1)} collective-permute-done((bf16[4,512,1,128]{3,1,2,0:T(8,128)(2,1)}, bf16[4,512,1,128]{3,1,2,0:T(8,128)(2,1)S(1)}, u32[]{:S(2)}, u32[]{:S(2)}) %collective-permute-start) | collective-permute-done | bytes 524320 | tf_op jit(solution)/shard_map/while/body/eval_jaxpr/ppermute | solution.py:12
  98.4 0.8 copy.28
  100.4 9.7 %collective-permute-done = bf16[4,512,1,128]{3,1,2,0:T(8,128)(2,1)S(1)} collective-permute-done((bf16[4,512,1,128]{3,1,2,0:T(8,128)(2,1)}, bf16[4,512,1,128]{3,1,2,0:T(8,128)(2,1)S(1)}, u32[]{:S(2)}, u32[]{:S(2)}) %collective-permute-start) | collective-permute-done | bytes 524320 | tf_op jit(solution)/shard_map/while/body/eval_jaxpr/ppermute | solution.py:12
  111.4 0.8 copy.28
  113.4 9.7 %collective-permute-done = bf16[4,512,1,128]{3,1,2,0:T(8,128)(2,1)S(1)} collective-permute-done((bf16[4,512,1,128]{3,1,2,0:T(8,128)(2,1)}, bf16[4,512,1,128]{3,1,2,0:T(8,128)(2,1)S(1)}, u32[]{:S(2)}, u32[]{:S(2)}) %collective-permute-start) | collective-permute-done | bytes 524320 | tf_op jit(solution)/shard_map/while/body/eval_jaxpr/ppermute | solution.py:12
  124.4 0.8 copy.28
  126.5 9.7 %collective-permute-done = bf16[4,512,1,128]{3,1,2,0:T(8,128)(2,1)S(1)} collective-permute-done((bf16[4,512,1,128]{3,1,2,0:T(8,128)(2,1)}, bf16[4,512,1,128]{3,1,2,0:T(8,128)(2,1)S(1)}, u32[]{:S(2)}, u32[]{:S(2)}) %collective-permute-start) | collective-permute-done | bytes 524320 | tf_op jit(solution)/shard_map/while/body/eval_jaxpr/ppermute | solution.py:12
  137.4 0.8 copy.28
  139.5 9.7 %collective-permute-done = bf16[4,512,1,128]{3,1,2,0:T(8,128)(2,1)S(1)} collective-permute-done((bf16[4,512,1,128]{3,1,2,0:T(8,128)(2,1)}, bf16[4,512,1,128]{3,1,2,0:T(8,128)(2,1)S(1)}, u32[]{:S(2)}, u32[]{:S(2)}) %collective-permute-start) | collective-permute-done | bytes 524320 | tf_op jit(solution)/shard_map/while/body/eval_jaxpr/ppermute | solution.py:12
  150.5 0.8 copy.28
  152.5 9.7 %collective-permute-done = bf16[4,512,1,128]{3,1,2,0:T(8,128)(2,1)S(1)} collective-permute-done((bf16[4,512,1,128]{3,1,2,0:T(8,128)(2,1)}, bf16[4,512,1,128]{3,1,2,0:T(8,128)(2,1)S(1)}, u32[]{:S(2)}, u32[]{:S(2)}) %collective-permute-start) | collective-permute-done | bytes 524320 | tf_op jit(solution)/shard_map/while/body/eval_jaxpr/ppermute | solution.py:12
  163.5 0.8 copy.28
  165.5 9.7 %collective-permute-done = bf16[4,512,1,128]{3,1,2,0:T(8,128)(2,1)S(1)} collective-permute-done((bf16[4,512,1,128]{3,1,2,0:T(8,128)(2,1)}, bf16[4,512,1,128]{3,1,2,0:T(8,128)(2,1)S(1)}, u32[]{:S(2)}, u32[]{:S(2)}) %collective-permute-start) | collective-permute-done | bytes 524320 | tf_op jit(solution)/shard_map/while/body/eval_jaxpr/ppermute | solution.py:12
  176.5 0.8 copy.28
  178.6 9.7 %collective-permute-done = bf16[4,512,1,128]{3,1,2,0:T(8,128)(2,1)S(1)} collective-permute-done((bf16[4,512,1,128]{3,1,2,0:T(8,128)(2,1)}, bf16[4,512,1,128]{3,1,2,0:T(8,128)(2,1)S(1)}, u32[]{:S(2)}, u32[]{:S(2)}) %collective-permute-start) | collective-permute-done | bytes 524320 | tf_op jit(solution)/shard_map/while/body/eval_jaxpr/ppermute | solution.py:12
  189.6 0.8 copy.28
  191.6 9.7 %collective-permute-done = bf16[4,512,1,128]{3,1,2,0:T(8,128)(2,1)S(1)} collective-permute-done((bf16[4,512,1,128]{3,1,2,0:T(8,128)(2,1)}, bf16[4,512,1,128]{3,1,2,0:T(8,128)(2,1)S(1)}, u32[]{:S(2)}, u32[]{:S(2)}) %collective-permute-start) | collective-permute-done | bytes 524320 | tf_op jit(solution)/shard_map/while/body/eval_jaxpr/ppermute | solution.py:12
  202.6 0.8 copy.28
  204.6 9.7 %collective-permute-done = bf16[4,512,1,128]{3,1,2,0:T(8,128)(2,1)S(1)} collective-permute-done((bf16[4,512,1,128]{3,1,2,0:T(8,128)(2,1)}, bf16[4,512,1,128]{3,1,2,0:T(8,128)(2,1)S(1)}, u32[]{:S(2)}, u32[]{:S(2)}) %collective-permute-start) | collective-permute-done | bytes 524320 | tf_op jit(solution)/shard_map/while/body/eval_jaxpr/ppermute | solution.py:12
  215.6 0.8 copy.28
  217.8 5.5 %fusion.31 = f32[2,512,2048]{2,1,0:T(8,128)} fusion(bf16[128,2048]{1,0:T(8,128)(2,1)} %param.9, bf16[1,512,128]{2,1,0:T(8,128)(2,1)S(1)} %get-tuple-element.99, bf16[1,512,128]{2,1,0:T(8,128)(2,1)S(1)} %get-tuple-element.98), kind=kOutput, calls=%fused_computation.55 | convolution fusion | flops 537001984 | bytes 9175040 | tf_op jit(solution)/shard_map/sqc,cd->sqd/dot_general | solution.py:82
  223.3 244.8 %reduce-scatter.2.cloned.1.call-done = f32[2,512,128]{2,1,0:T(8,128)} async-done(((f32[2,512,2048]{2,1,0:T(8,128)}), f32[2,512,128]{2,1,0:T(8,128)}) %reduce-scatter.2.cloned.1.call-update) | async-done | bytes 524304 | tf_op jit(solution)/shard_map/reduce_scatter | solution.py:83
  468.1 1.1 convert.11
  469.2 0.7 slice_bitcast_fusion.10
  (197 shorter events, 38.8 us)
Async XLA Ops:
  7.2 1.6 copy-start
  7.2 460.9 %reduce-scatter.2.cloned.1.call-start = ((), (), s32[]{:S(2)}) async-start(), calls=%async_computation.1 | async-start | bytes 8912896 | tf_op jit(solution)/shard_map/reduce_scatter | solution.py:83
  8.8 1.9 copy-start.3
  11.4 1.6 copy-start.2
  15.1 1.2 copy-start.1
  22.2 9.7 %collective-permute-start = (bf16[4,512,1,128]{3,1,2,0:T(8,128)(2,1)}, bf16[4,512,1,128]{3,1,2,0:T(8,128)(2,1)S(1)}, u32[]{:S(2)}, u32[]{:S(2)}) collective-permute-start(bf16[4,512,1,128]{3,1,2,0:T(8,128)(2,1)} %get-tuple-element.190), channel_id=1, source_target_pairs={{0,16},{16,32},{32,48},{48,64},{64,80},{80,96},{96,112},{112,128},... | collective-permute-start | bytes 1572872 | tf_op jit(solution)/shard_map/while/body/eval_jaxpr/ppermute | solution.py:12
  35.2 9.8 %collective-permute-start = (bf16[4,512,1,128]{3,1,2,0:T(8,128)(2,1)}, bf16[4,512,1,128]{3,1,2,0:T(8,128)(2,1)S(1)}, u32[]{:S(2)}, u32[]{:S(2)}) collective-permute-start(bf16[4,512,1,128]{3,1,2,0:T(8,128)(2,1)} %get-tuple-element.190), channel_id=1, source_target_pairs={{0,16},{16,32},{32,48},{48,64},{64,80},{80,96},{96,112},{112,128},... | collective-permute-start | bytes 1572872 | tf_op jit(solution)/shard_map/while/body/eval_jaxpr/ppermute | solution.py:12
  48.2 9.8 %collective-permute-start = (bf16[4,512,1,128]{3,1,2,0:T(8,128)(2,1)}, bf16[4,512,1,128]{3,1,2,0:T(8,128)(2,1)S(1)}, u32[]{:S(2)}, u32[]{:S(2)}) collective-permute-start(bf16[4,512,1,128]{3,1,2,0:T(8,128)(2,1)} %get-tuple-element.190), channel_id=1, source_target_pairs={{0,16},{16,32},{32,48},{48,64},{64,80},{80,96},{96,112},{112,128},... | collective-permute-start | bytes 1572872 | tf_op jit(solution)/shard_map/while/body/eval_jaxpr/ppermute | solution.py:12
  61.2 9.8 %collective-permute-start = (bf16[4,512,1,128]{3,1,2,0:T(8,128)(2,1)}, bf16[4,512,1,128]{3,1,2,0:T(8,128)(2,1)S(1)}, u32[]{:S(2)}, u32[]{:S(2)}) collective-permute-start(bf16[4,512,1,128]{3,1,2,0:T(8,128)(2,1)} %get-tuple-element.190), channel_id=1, source_target_pairs={{0,16},{16,32},{32,48},{48,64},{64,80},{80,96},{96,112},{112,128},... | collective-permute-start | bytes 1572872 | tf_op jit(solution)/shard_map/while/body/eval_jaxpr/ppermute | solution.py:12
  74.3 9.8 %collective-permute-start = (bf16[4,512,1,128]{3,1,2,0:T(8,128)(2,1)}, bf16[4,512,1,128]{3,1,2,0:T(8,128)(2,1)S(1)}, u32[]{:S(2)}, u32[]{:S(2)}) collective-permute-start(bf16[4,512,1,128]{3,1,2,0:T(8,128)(2,1)} %get-tuple-element.190), channel_id=1, source_target_pairs={{0,16},{16,32},{32,48},{48,64},{64,80},{80,96},{96,112},{112,128},... | collective-permute-start | bytes 1572872 | tf_op jit(solution)/shard_map/while/body/eval_jaxpr/ppermute | solution.py:12
  87.3 9.8 %collective-permute-start = (bf16[4,512,1,128]{3,1,2,0:T(8,128)(2,1)}, bf16[4,512,1,128]{3,1,2,0:T(8,128)(2,1)S(1)}, u32[]{:S(2)}, u32[]{:S(2)}) collective-permute-start(bf16[4,512,1,128]{3,1,2,0:T(8,128)(2,1)} %get-tuple-element.190), channel_id=1, source_target_pairs={{0,16},{16,32},{32,48},{48,64},{64,80},{80,96},{96,112},{112,128},... | collective-permute-start | bytes 1572872 | tf_op jit(solution)/shard_map/while/body/eval_jaxpr/ppermute | solution.py:12
  100.3 9.8 %collective-permute-start = (bf16[4,512,1,128]{3,1,2,0:T(8,128)(2,1)}, bf16[4,512,1,128]{3,1,2,0:T(8,128)(2,1)S(1)}, u32[]{:S(2)}, u32[]{:S(2)}) collective-permute-start(bf16[4,512,1,128]{3,1,2,0:T(8,128)(2,1)} %get-tuple-element.190), channel_id=1, source_target_pairs={{0,16},{16,32},{32,48},{48,64},{64,80},{80,96},{96,112},{112,128},... | collective-permute-start | bytes 1572872 | tf_op jit(solution)/shard_map/while/body/eval_jaxpr/ppermute | solution.py:12
  113.3 9.8 %collective-permute-start = (bf16[4,512,1,128]{3,1,2,0:T(8,128)(2,1)}, bf16[4,512,1,128]{3,1,2,0:T(8,128)(2,1)S(1)}, u32[]{:S(2)}, u32[]{:S(2)}) collective-permute-start(bf16[4,512,1,128]{3,1,2,0:T(8,128)(2,1)} %get-tuple-element.190), channel_id=1, source_target_pairs={{0,16},{16,32},{32,48},{48,64},{64,80},{80,96},{96,112},{112,128},... | collective-permute-start | bytes 1572872 | tf_op jit(solution)/shard_map/while/body/eval_jaxpr/ppermute | solution.py:12
  126.4 9.8 %collective-permute-start = (bf16[4,512,1,128]{3,1,2,0:T(8,128)(2,1)}, bf16[4,512,1,128]{3,1,2,0:T(8,128)(2,1)S(1)}, u32[]{:S(2)}, u32[]{:S(2)}) collective-permute-start(bf16[4,512,1,128]{3,1,2,0:T(8,128)(2,1)} %get-tuple-element.190), channel_id=1, source_target_pairs={{0,16},{16,32},{32,48},{48,64},{64,80},{80,96},{96,112},{112,128},... | collective-permute-start | bytes 1572872 | tf_op jit(solution)/shard_map/while/body/eval_jaxpr/ppermute | solution.py:12
  139.4 9.8 %collective-permute-start = (bf16[4,512,1,128]{3,1,2,0:T(8,128)(2,1)}, bf16[4,512,1,128]{3,1,2,0:T(8,128)(2,1)S(1)}, u32[]{:S(2)}, u32[]{:S(2)}) collective-permute-start(bf16[4,512,1,128]{3,1,2,0:T(8,128)(2,1)} %get-tuple-element.190), channel_id=1, source_target_pairs={{0,16},{16,32},{32,48},{48,64},{64,80},{80,96},{96,112},{112,128},... | collective-permute-start | bytes 1572872 | tf_op jit(solution)/shard_map/while/body/eval_jaxpr/ppermute | solution.py:12
  152.4 9.8 %collective-permute-start = (bf16[4,512,1,128]{3,1,2,0:T(8,128)(2,1)}, bf16[4,512,1,128]{3,1,2,0:T(8,128)(2,1)S(1)}, u32[]{:S(2)}, u32[]{:S(2)}) collective-permute-start(bf16[4,512,1,128]{3,1,2,0:T(8,128)(2,1)} %get-tuple-element.190), channel_id=1, source_target_pairs={{0,16},{16,32},{32,48},{48,64},{64,80},{80,96},{96,112},{112,128},... | collective-permute-start | bytes 1572872 | tf_op jit(solution)/shard_map/while/body/eval_jaxpr/ppermute | solution.py:12
  165.4 9.8 %collective-permute-start = (bf16[4,512,1,128]{3,1,2,0:T(8,128)(2,1)}, bf16[4,512,1,128]{3,1,2,0:T(8,128)(2,1)S(1)}, u32[]{:S(2)}, u32[]{:S(2)}) collective-permute-start(bf16[4,512,1,128]{3,1,2,0:T(8,128)(2,1)} %get-tuple-element.190), channel_id=1, source_target_pairs={{0,16},{16,32},{32,48},{48,64},{64,80},{80,96},{96,112},{112,128},... | collective-permute-start | bytes 1572872 | tf_op jit(solution)/shard_map/while/body/eval_jaxpr/ppermute | solution.py:12
  178.5 9.8 %collective-permute-start = (bf16[4,512,1,128]{3,1,2,0:T(8,128)(2,1)}, bf16[4,512,1,128]{3,1,2,0:T(8,128)(2,1)S(1)}, u32[]{:S(2)}, u32[]{:S(2)}) collective-permute-start(bf16[4,512,1,128]{3,1,2,0:T(8,128)(2,1)} %get-tuple-element.190), channel_id=1, source_target_pairs={{0,16},{16,32},{32,48},{48,64},{64,80},{80,96},{96,112},{112,128},... | collective-permute-start | bytes 1572872 | tf_op jit(solution)/shard_map/while/body/eval_jaxpr/ppermute | solution.py:12
  191.5 9.8 %collective-permute-start = (bf16[4,512,1,128]{3,1,2,0:T(8,128)(2,1)}, bf16[4,512,1,128]{3,1,2,0:T(8,128)(2,1)S(1)}, u32[]{:S(2)}, u32[]{:S(2)}) collective-permute-start(bf16[4,512,1,128]{3,1,2,0:T(8,128)(2,1)} %get-tuple-element.190), channel_id=1, source_target_pairs={{0,16},{16,32},{32,48},{48,64},{64,80},{80,96},{96,112},{112,128},... | collective-permute-start | bytes 1572872 | tf_op jit(solution)/shard_map/while/body/eval_jaxpr/ppermute | solution.py:12
  204.5 9.8 %collective-permute-start = (bf16[4,512,1,128]{3,1,2,0:T(8,128)(2,1)}, bf16[4,512,1,128]{3,1,2,0:T(8,128)(2,1)S(1)}, u32[]{:S(2)}, u32[]{:S(2)}) collective-permute-start(bf16[4,512,1,128]{3,1,2,0:T(8,128)(2,1)} %get-tuple-element.190), channel_id=1, source_target_pairs={{0,16},{16,32},{32,48},{48,64},{64,80},{80,96},{96,112},{112,128},... | collective-permute-start | bytes 1572872 | tf_op jit(solution)/shard_map/while/body/eval_jaxpr/ppermute | solution.py:12
Sparse Core Ops, SparseCore 0:
  223.4 244.6 reduce-scatter.1
where the time goes:
time: 477 us
  waiting for transfers between devices  390 us (82%)
  matrix products  46.3 us (10%)
  local copies, waits for them, and re-layouts  16.2 us (3%)
  between operations  14.2 us (3%)
  other arithmetic  7.46 us (2%)
    reduce_scatter x1, waiting for transfers between devices, local(): lax.psum_scatter(partial_terms, 'head', scatter_dimension=2, tiled=True)  245 us
    ppermute x15, waiting for transfers between devices, shifted(): return lax.ppermute(value, axis, pairs)  146 us
    while x30, local copies, waits for them, and re-layouts  11.9 us
  transfers between devices with their start and end apart: 16, of which 16 were waited for; matrix products, arithmetic and copies ran while one was open for 0% of the time, Pallas kernels for 0%

commit v1 on v0

v1 whole, which is shorter than its diff:
```python
import functools
import math

import jax
import jax.numpy as jnp
from jax import lax
from jax.experimental import pallas as pl
from jax.experimental.pallas import tpu as pltpu
from jax.sharding import PartitionSpec as P

F32 = jnp.float32
BF16 = jnp.bfloat16
MESH = pl.DeviceIdType.MESH
HD = 128
D = 2048
TOK = 512
HALF = TOK // 2
NY, NX, NC = 4, 2, 2
NH, NZ = 2, 8
PIECE = TOK // NZ
LOG2E = math.log2(math.e)
LN2 = math.log(2.0)
SCALE = HD ** (-0.5)
ORDER = (4, 3, 5, 2, 6, 1, 7, 0)


def dot(a, b):
    return jnp.dot(a, b, preferred_element_type=F32)


def dot_nt(a, b):
    return lax.dot_general(a, b, (((1,), (1,)), ((), ())), preferred_element_type=F32)


def lane_sum(value):
    parts = [value[:, i : i + 128] for i in range(0, value.shape[1], 128)]
    return functools.reduce(lambda a, b: a + b, parts)


def kernel(
    x_hbm, t_hbm, wqkv_hbm, wout_hbm, out_ref, tout_ref,
    xt, wq, kv, qq, acc, top, total, spread,
    part_out, part_in, stat_out, stat_in, own_part, coef,
    a_out, a_in, w_all, f_out, f_in,
    ld, kv_s, kv_r, sib_s, sib_r, q_sem, w_s, w_r, ws_s, ws_r,
    p_s, p_r, st_sem, a_s, a_r, f_s, f_r,
):
    ctx = lax.axis_index("ctx")
    head = lax.axis_index("head")
    y, x, core = ctx // 4, (ctx // 2) % 2, ctx % 2
    xh, z = head // 8, head % 8

    def peer(dy=0, dx=0, dc=0, dh=0, dz=0):
        ny = lax.rem(y + (dy + NY), NY)
        nx = lax.rem(x + dx, NX)
        nc = lax.rem(core + dc, NC)
        nh = lax.rem(xh + dh, NH)
        nz = lax.rem(z + (dz + NZ), NZ)
        return ((ny * NX + nx) * NC + nc, nh * NZ + nz)

    def remote(src, dst, send, recv, device):
        return pltpu.make_async_remote_copy(
            src_ref=src, dst_ref=dst, send_sem=send, recv_sem=recv, device_id=device, device_id_type=MESH
        )

    friends = [peer(dc=1), peer(dx=1), peer(dy=1), peer(dy=-1)]
    friends += [peer(dh=b, dz=k) for b in range(NH) for k in range(NZ) if (b, k) != (0, 0)]
    barrier = pltpu.get_barrier_semaphore()
    for friend in friends:
        pl.semaphore_signal(barrier, inc=1, device_id=friend, device_id_type=MESH)

    def load(src, dst, index):
        copy = pltpu.make_async_copy(src, dst, ld.at[index])
        copy.start()
        return copy

    ld_k = load(wqkv_hbm.at[1], wq.at[:, 0:128], 0)
    ld_v = load(wqkv_hbm.at[2], wq.at[:, 128:256], 1)
    ld_x = [None, None]
    ld_t = [None, None]
    for h in range(2):
        rows = pl.ds(h * HALF, HALF)
        ld_x[h] = load(x_hbm.at[rows], xt.at[pl.ds(h * HALF, HALF)], 2 + h)
        ld_t[h] = load(t_hbm.at[rows], xt.at[pl.ds(TOK + h * HALF, HALF)], 4 + h)
    ld_q = load(wqkv_hbm.at[0], wq.at[:, 256:384], 6)
    ld_w = load(wout_hbm, w_all.at[0], 7)

    sends = []

    def start(copy):
        copy.start()
        sends.append(copy)
        return copy

    def project_kv(h):
        rows = pl.ds(h * 2 * HALF, HALF)
        ld_x[h].wait()
        both = dot(xt[pl.ds(h * HALF, HALF), :], wq[:, 0:256])
        kv[0, rows, 0:128] = both[:, 0:128].astype(BF16)
        kv[0, rows, 256:384] = both[:, 128:256].astype(BF16)
        ld_t[h].wait()
        both = dot(xt[pl.ds(TOK + h * HALF, HALF), :], wq[:, 0:256])
        kv[0, rows, 128:256] = (both[:, 0:128] * LN2).astype(BF16)
        kv[0, rows, 384:512] = both[:, 128:256].astype(BF16)

    def block(r, h):
        return kv.at[r, pl.ds(h * 2 * HALF, HALF)]

    def share(r, h):
        dst = kv.at[r, pl.ds(h * 2 * HALF + HALF, HALF)]
        return start(remote(block(r, h), dst, sib_s.at[r, h], sib_r.at[r, h], peer(dc=1)))

    def plus(r, h, index):
        to = (r + NY - 1) % NY
        return start(remote(block(r, h), block(to, h), kv_s.at[index], kv_r.at[to, h], peer(dy=1)))

    def minus(r, h, index):
        to = (r + 1) % NY
        return start(remote(block(r, h), block(to, h), kv_s.at[index], kv_r.at[to, h], peer(dy=-1)))

    def kv_arrived(r, h):
        remote(block(r, h), block(r, h), kv_s.at[0], kv_r.at[r, h], peer(dy=1)).wait_recv()

    def shared(r, h):
        dst = kv.at[r, pl.ds(h * 2 * HALF + HALF, HALF)]
        remote(dst, dst, sib_s.at[r, h], sib_r.at[r, h], peer(dc=1)).wait_recv()

    half_rows = pl.ds(pl.multiple_of(core * 64, 64), 64)

    def w_right(hop):
        rows = half_rows if hop < 3 else pl.ds(pl.multiple_of(core * 64, 64), 32)
        src, to = (NZ - hop) % NZ, NZ - 1 - hop
        start(remote(w_all.at[src, rows], w_all.at[to, rows], w_s.at[hop], w_r.at[to], peer(dz=1)))

    def w_left(hop):
        rows = half_rows if hop < 3 else pl.ds(pl.multiple_of(core * 64 + 32, 32), 32)
        src, to = hop, hop + 1
        sem = w_r.at[to] if hop < 3 else w_r.at[0]
        start(remote(w_all.at[src, rows], w_all.at[to, rows], w_s.at[4 + hop], sem, peer(dz=-1)))

    def w_arrived(slot):
        if slot == 4:
            rows = pl.ds(pl.multiple_of(core * 64, 64), 32)
            dst = w_all.at[4, rows]
            remote(dst, dst, w_s.at[0], w_r.at[4], peer(dz=1)).wait_recv()
            rows = pl.ds(pl.multiple_of(core * 64 + 32, 32), 32)
            dst = w_all.at[4, rows]
            remote(dst, dst, w_s.at[0], w_r.at[0], peer(dz=1)).wait_recv()
        else:
            dst = w_all.at[slot, half_rows]
            remote(dst, dst, w_s.at[0], w_r.at[slot], peer(dz=1)).wait_recv()
        src = w_all.at[slot, half_rows]
        start(remote(src, src, ws_s.at[slot], ws_r.at[slot], peer(dc=1)))

    def w_shared(slot):
        rows = pl.ds(pl.multiple_of((1 - core) * 64, 64), 64)
        dst = w_all.at[slot, rows]
        remote(dst, dst, ws_s.at[slot], ws_r.at[slot], peer(dc=1)).wait_recv()

    def w_hop(hop):
        w_arrived(NZ - hop)
        w_right(hop)
        w_arrived(hop)
        w_left(hop)

    def attend(lo, rows, r, key_lo, keys, first=False):
        rs = pl.ds(lo, rows)
        ks = pl.ds(key_lo, keys)
        scores = dot_nt(qq[rs, 128:256], kv[r, ks, 0:128])
        tscores = dot_nt(qq[rs, :], kv[r, ks, 0:256])
        peak = jnp.max(scores, axis=1, keepdims=True)
        if first:
            new_top = jnp.broadcast_to(peak, (rows, 128))
        else:
            old_top = top[rs, :]
            new_top = jnp.maximum(old_top, peak)
            factor = jnp.exp2(old_top - new_top)
        top[rs, :] = new_top
        weights = jnp.exp2(scores - new_top[:, 0:1])
        mixed = weights * tscores
        sum_w, sum_m = lane_sum(weights), lane_sum(mixed)
        add = dot(weights.astype(BF16), kv[r, ks, 256:512])
        add_m = dot(mixed.astype(BF16), kv[r, ks, 256:384])
        add_t = add[:, 128:256] + add_m
        if first:
            total[rs, :] = sum_w
            spread[rs, :] = sum_m
            acc[rs, 0:128] = add[:, 0:128]
            acc[rs, 128:256] = add_t
        else:
            total[rs, :] = total[rs, :] * factor + sum_w
            spread[rs, :] = spread[rs, :] * factor + sum_m
            acc[rs, 0:128] = acc[rs, 0:128] * factor + add[:, 0:128]
            acc[rs, 128:256] = acc[rs, 128:256] * factor + add_t

    def finish(lo):
        rs = pl.ds(lo, TOK)
        weight = jnp.sum(total[rs, :], axis=1, keepdims=True)
        inverse = 1.0 / weight
        mean = jnp.sum(spread[rs, :], axis=1, keepdims=True) * inverse
        out = acc[rs, 0:128] * inverse
        tangent = acc[rs, 128:256] * inverse - mean * out
        return out, tangent, top[rs, 0:1], weight, mean

    ld_k.wait()
    ld_v.wait()
    project_kv(0)
    pl.semaphore_wait(barrier, len(friends))
    plus(0, 0, 0)
    share(0, 0)
    project_kv(1)
    minus(0, 1, 3)
    plus(0, 1, 1)
    minus(0, 0, 4)
    share(0, 1)
    ld_w.wait()
    w_right(0)
    w_left(0)
    ld_q.wait()
    qq[TOK : 2 * TOK, 128:256] = (dot(xt[0:TOK, :], wq[:, 256:384]) * (SCALE * LOG2E)).astype(BF16)
    qq[TOK : 2 * TOK, 0:128] = (dot(xt[TOK : 2 * TOK, :], wq[:, 256:384]) * SCALE).astype(BF16)
    q_copy = start(remote(qq.at[pl.ds(TOK, TOK)], qq.at[pl.ds(0, TOK)], q_sem.at[0], q_sem.at[1], peer(dx=1)))

    shared(0, 0)
    shared(0, 1)
    attend(TOK, TOK, 0, 0, 1024, first=True)
    kv_arrived(3, 0)
    plus(3, 0, 2)
    share(3, 0)
    kv_arrived(1, 1)
    minus(1, 1, 5)
    share(1, 1)
    q_copy.wait_recv()
    attend(0, TOK, 0, 0, 1024, first=True)
    w_hop(1)
    shared(3, 0)
    attend(0, 2 * TOK, 3, 0, 512)
    shared(1, 1)
    attend(0, 2 * TOK, 1, 512, 512)
    kv_arrived(3, 1)
    share(3, 1)
    kv_arrived(1, 0)
    share(1, 0)
    w_hop(2)
    shared(3, 1)
    attend(0, 2 * TOK, 3, 512, 512)
    shared(1, 0)
    attend(0, 2 * TOK, 1, 0, 512)
    kv_arrived(2, 0)
    share(2, 0)
    kv_arrived(2, 1)
    share(2, 1)
    w_hop(3)
    shared(2, 0)
    attend(0, 2 * TOK, 2, 0, 512)
    shared(2, 1)
    attend(0, TOK, 2, 512, 512)

    out, tangent, peak, weight, mean = finish(0)
    part_out[:, 0:128] = out.astype(BF16)
    part_out[:, 128:256] = tangent.astype(BF16)
    lane = lax.broadcasted_iota(jnp.int32, (TOK, 128), 1)
    stats = jnp.where(lane == 0, peak, jnp.where(lane == 1, weight, mean))
    stat_out[...] = jnp.transpose(stats)[0:8, :]
    stat_copy = start(remote(stat_out, stat_in, st_sem.at[0], st_sem.at[1], peer(dx=1)))

    def piece(k):
        return pl.ds(pl.multiple_of(lax.rem(z + k, NZ) * PIECE, PIECE), PIECE)

    part_copies = {}
    for k in ORDER:
        rows = piece(k)
        part_copies[k] = start(remote(part_out.at[rows], part_in.at[rows], p_s.at[k], p_r.at[k], peer(dx=1)))
    attend(TOK, TOK, 2, 512, 512)
    out, tangent, peak, weight, mean = finish(TOK)
    own_part[:, 0:128] = out
    own_part[:, 128:256] = tangent
    stat_copy.wait_recv()
    padded = jnp.concatenate([stat_in[...], jnp.zeros((120, TOK), F32)], axis=0)
    other = jnp.transpose(padded)
    peak2, weight2, mean2 = other[:, 0:1], other[:, 1:2], other[:, 2:3]
    high = jnp.maximum(peak, peak2)
    mass = weight * jnp.exp2(peak - high)
    mass2 = weight2 * jnp.exp2(peak2 - high)
    inverse = 1.0 / (mass + mass2)
    p1, p2 = mass * inverse, mass2 * inverse
    coef[0] = jnp.broadcast_to(p1, (TOK, 128))
    coef[1] = jnp.broadcast_to(p2, (TOK, 128))
    coef[2] = jnp.broadcast_to(p1 * p2 * (mean - mean2), (TOK, 128))

    a_copies = {}
    for k in ORDER:
        rows = piece(k)
        part_copies[k].wait_recv()
        o1, u1 = own_part[rows, 0:128], own_part[rows, 128:256]
        o2, u2 = part_in[rows, 0:128].astype(F32), part_in[rows, 128:256].astype(F32)
        c1, c2, c3 = coef[0, rows, :], coef[1, rows, :], coef[2, rows, :]
        merged = (c1 * o1 + c2 * o2).astype(BF16)
        tmerged = (c1 * u1 + c2 * u2 + c3 * (o1 - o2)).astype(BF16)
        if k == 0:
            a_in[0:PIECE, 0:128] = merged
            a_in[PIECE : 2 * PIECE, 0:128] = tmerged
        else:
            a_out[k, 0:PIECE, :] = merged
            a_out[k, PIECE : 2 * PIECE, :] = tmerged
            back = NZ - k
            dst = a_in.at[:, back * 128 : back * 128 + 128]
            a_copies[k] = start(remote(a_out.at[k], dst, a_s.at[k], a_r.at[back], peer(dz=k)))

    w_arrived(4)
    for slot in range(1, NZ):
        w_shared(slot)
    for k in range(1, NZ):
        a_copies[k].wait_recv()

    f_copies = {}
    for k in ORDER:
        for b in (1, 0):
            column = (lax.rem(xh + b, NH) * NZ + lax.rem(z + k, NZ)) * 128
            rhs = w_all[:, :, pl.ds(pl.multiple_of(column, 128), 128)].reshape(NZ * 128, 128)
            term = dot(a_in[...], rhs).astype(BF16)
            if (b, k) == (0, 0):
                f_in[0, 0] = term
            else:
                f_out[b, k] = term
                back = (NZ - k) % NZ
                f_copies[b, k] = start(
                    remote(f_out.at[b, k], f_in.at[b, back], f_s.at[b, k], f_r.at[b, back], peer(dh=b, dz=k))
                )
    for k in range(NZ):
        for b in range(NH):
            if (b, k) != (0, 0):
                remote(f_out.at[b, k], f_in.at[b, k], f_s.at[b, k], f_r.at[b, k], peer(dh=b, dz=k)).wait_recv()
        rows = piece(k)
        summed = f_in[0, k].astype(F32) + f_in[1, k].astype(F32)
        out_ref[rows, :] = summed[0:PIECE].astype(BF16)
        tout_ref[rows, :] = summed[PIECE : 2 * PIECE].astype(BF16)
    for copy in sends:
        copy.wait_send()


def local(inputs, tangents, w_qkv, w_out):
    dma = pltpu.SemaphoreType.DMA
    vmem = pltpu.VMEM
    return pl.pallas_call(
        kernel,
        name="tangent_attention",
        out_shape=[jax.ShapeDtypeStruct((TOK, 128), BF16)] * 2,
        in_specs=[pl.BlockSpec(memory_space=pl.ANY)] * 4,
        out_specs=[pl.BlockSpec(memory_space=pltpu.VMEM)] * 2,
        scratch_shapes=[
            vmem((2 * TOK, D), BF16),
            vmem((D, 384), BF16),
            vmem((NY, 1024, 512), BF16),
            vmem((2 * TOK, 256), BF16),
            vmem((2 * TOK, 256), F32),
            vmem((2 * TOK, 128), F32),
            vmem((2 * TOK, 128), F32),
            vmem((2 * TOK, 128), F32),
            vmem((TOK, 256), BF16),
            vmem((TOK, 256), BF16),
            vmem((8, TOK), F32),
            vmem((8, TOK), F32),
            vmem((TOK, 256), F32),
            vmem((3, TOK, 128), F32),
            vmem((NZ, 128, 128), BF16),
            vmem((128, NZ * 128), BF16),
            vmem((NZ, 128, D), BF16),
            vmem((NH, NZ, 128, 128), BF16),
            vmem((NH, NZ, 128, 128), BF16),
            dma((8,)),
            dma((6,)),
            dma((NY, 2)),
            dma((NY, 2)),
            dma((NY, 2)),
            dma((2,)),
            dma((8,)),
            dma((8,)),
            dma((8,)),
            dma((8,)),
            dma((8,)),
            dma((8,)),
            dma((2,)),
            dma((8,)),
            dma((8,)),
            dma((NH, NZ)),
            dma((NH, NZ)),
        ],
        compiler_params=pltpu.CompilerParams(
            collective_id=0, has_side_effects=True, vmem_limit_bytes=58 * 2**20
        ),
    )(inputs, tangents, w_qkv, w_out)


def solution(mesh):
    return jax.shard_map(
        local,
        mesh=mesh,
        in_specs=(P("ctx", None), P("ctx", None), P(None, None, "head"), P("head", None)),
        out_specs=(P("ctx", "head"), P("ctx", "head")),
        check_vma=False,
    )
```

time: 477 us -> 65.8 us (0.14)
  waiting for transfers between devices: 390 us -> 0 us
  Pallas kernels: 0 us -> 61.6 us
  matrix products: 46.3 us -> 0 us
  between operations: 14.2 us -> 0.64 us
  local copies, waits for them, and re-layouts: 16.2 us -> 3.14 us
  other arithmetic: 7.46 us -> 0 us
    reduce_scatter x1 -> x0, waiting for transfers between devices: 245 us -> none  [local(): lax.psum_scatter(partial_terms, 'head', scatter_dimension=2, tiled=True)]
    ppermute x15 -> x0, waiting for transfers between devices: 146 us -> none  [shifted(): return lax.ppermute(value, axis, pairs)]
    pallas_call x0 -> x1, Pallas kernels: none -> 61.6 us  [local(): pl.pallas_call(kernel, name='tangent_attention', out_shape=[jax.ShapeDtyp...]
    dot_general x103 -> x0, matrix products: 46.3 us -> none  [the longest x16 6.72 us: absorb(): jnp.einsum('qhk,khd->qhd', mixed_b, values, preferred_element_type=jnp.fl...]
    while x32 -> x0, local copies, waits for them, and re-layouts: 13.1 us -> none
  transfers between devices with their start and end apart: 16 -> 0, of which waited for: 16 -> 0; matrix products, arithmetic and copies ran while one was open for 0% -> 0% of each run, Pallas kernels for 0% -> 0%
where the time goes in v1:
time: 65.8 us; the launch traced here: 65.3 us
  Pallas kernels  61.6 us (94%)
  local copies, waits for them, and re-layouts  3.14 us (5%)
    pallas_call x1, Pallas kernels, local(): pl.pallas_call(kernel, name='tangent_attention', out_shape=[jax.ShapeDtyp...  61.6 us
    unnamed x2, local copies, waits for them, and re-layouts  3.14 us

profile of v1, /device:TPU:8, one launch (start us, length us, event | category | flops | bytes accessed | tf_op | source)
XLA Modules:
  0.0 65.3 jit_solution(16391382223089214533)
XLA Ops:
  0.6 61.6 %tangent_attention.1 = (bf16[512,128]{1,0:T(8,128)(2,1)}, bf16[512,128]{1,0:T(8,128)(2,1)}) custom-call(bf16[512,2048]{1,0:T(8,128)(2,1)} %x_hbm.1, bf16[512,2048]{1,0:T(8,128)(2,1)} %t_hbm.1, bf16[3,2048,128]{2,1,0:T(8,128)(2,1)} %wqkv_hbm.1, bf16[128,2048]{1,0:T(8,128)(2,1)} %wout_hbm.1), custom_call_target="tpu_custom_call" | custom-call | tf_op jit(solution)/shard_map/tangent_attention/pallas_call | solution.py:345
  62.2 1.6 %copy.8 = bf16[512,128]{1,0:T(8,128)(2,1)} copy(bf16[512,128]{1,0:T(8,128)(2,1)} %get-tuple-element.4) | data formatting | bytes 262144
  63.8 1.6 %copy.9 = bf16[512,128]{1,0:T(8,128)(2,1)} copy(bf16[512,128]{1,0:T(8,128)(2,1)} %get-tuple-element.5) | data formatting | bytes 262144

commit v2 on v1

--- a/solution.py
+++ b/solution.py
@@ -38,12 +38,12 @@
 
 
 def kernel(
-    x_hbm, t_hbm, wqkv_hbm, wout_hbm, out_ref, tout_ref,
+    x_hbm, t_hbm, wqkv_hbm, wout_hbm, result,
     xt, wq, kv, qq, acc, top, total, spread,
     part_out, part_in, stat_out, stat_in, own_part, coef,
-    a_out, a_in, w_all, f_out, f_in,
+    a_out, a_in, w_all, g_out, g_in, g_own, f_out,
     ld, kv_s, kv_r, sib_s, sib_r, q_sem, w_s, w_r, ws_s, ws_r,
-    p_s, p_r, st_sem, a_s, a_r, f_s, f_r,
+    p_s, p_r, st_sem, a_s, a_r, g_s, g_r, f_s, f_r,
 ):
     ctx = lax.axis_index("ctx")
     head = lax.axis_index("head")
@@ -64,7 +64,7 @@
         )
 
     friends = [peer(dc=1), peer(dx=1), peer(dy=1), peer(dy=-1)]
-    friends += [peer(dh=b, dz=k) for b in range(NH) for k in range(NZ) if (b, k) != (0, 0)]
+    friends += [peer(dz=k) for k in range(1, NZ)] + [peer(dh=1)]
     barrier = pltpu.get_barrier_semaphore()
     for friend in friends:
         pl.semaphore_signal(barrier, inc=1, device_id=friend, device_id_type=MESH)
@@ -80,63 +80,66 @@
     ld_t = [None, None]
     for h in range(2):
         rows = pl.ds(h * HALF, HALF)
-        ld_x[h] = load(x_hbm.at[rows], xt.at[pl.ds(h * HALF, HALF)], 2 + h)
-        ld_t[h] = load(t_hbm.at[rows], xt.at[pl.ds(TOK + h * HALF, HALF)], 4 + h)
+        ld_x[h] = load(x_hbm.at[rows], xt.at[pl.ds(2 * h * HALF, HALF)], 2 + h)
+        ld_t[h] = load(t_hbm.at[rows], xt.at[pl.ds(2 * h * HALF + HALF, HALF)], 4 + h)
+    ld_w = load(wout_hbm, w_all.at[0], 7)
     ld_q = load(wqkv_hbm.at[0], wq.at[:, 256:384], 6)
-    ld_w = load(wout_hbm, w_all.at[0], 7)
-
-    sends = []
 
     def start(copy):
         copy.start()
-        sends.append(copy)
         return copy
+
+    def sent(sem, src):
+        remote(src, src, sem, q_sem.at[1], peer(dc=1)).wait_send()
 
     def project_kv(h):
         rows = pl.ds(h * 2 * HALF, HALF)
         ld_x[h].wait()
-        both = dot(xt[pl.ds(h * HALF, HALF), :], wq[:, 0:256])
-        kv[0, rows, 0:128] = both[:, 0:128].astype(BF16)
-        kv[0, rows, 256:384] = both[:, 128:256].astype(BF16)
         ld_t[h].wait()
-        both = dot(xt[pl.ds(TOK + h * HALF, HALF), :], wq[:, 0:256])
-        kv[0, rows, 128:256] = (both[:, 0:128] * LN2).astype(BF16)
-        kv[0, rows, 384:512] = both[:, 128:256].astype(BF16)
+        flat = dot(xt[pl.ds(h * 2 * HALF, HALF), :], wq[:, 0:256])
+        tflat = dot(xt[pl.ds(h * 2 * HALF + HALF, HALF), :], wq[:, 0:256])
+        kv[0, rows, 0:128] = flat[:, 0:128].astype(BF16)
+        kv[0, rows, 256:384] = flat[:, 128:256].astype(BF16)
+        kv[0, rows, 128:256] = (tflat[:, 0:128] * LN2).astype(BF16)
+        kv[0, rows, 384:512] = tflat[:, 128:256].astype(BF16)
 
     def block(r, h):
-        return kv.at[r, pl.ds(h * 2 * HALF, HALF)]
+        return kv.at[r, pl.ds(h * HALF if r == 2 else h * 2 * HALF, HALF)]
+
+    def other(r, h):
+        return kv.at[r, pl.ds(h * HALF + 2 * HALF if r == 2 else h * 2 * HALF + HALF, HALF)]
 
     def share(r, h):
-        dst = kv.at[r, pl.ds(h * 2 * HALF + HALF, HALF)]
-        return start(remote(block(r, h), dst, sib_s.at[r, h], sib_r.at[r, h], peer(dc=1)))
-
-    def plus(r, h, index):
+        dst = other(r, h)
+        return start(remote(block(r, h), dst, sib_s.at[0], sib_r.at[r, h], peer(dc=1)))
+
+    def plus(r, h):
         to = (r + NY - 1) % NY
-        return start(remote(block(r, h), block(to, h), kv_s.at[index], kv_r.at[to, h], peer(dy=1)))
-
-    def minus(r, h, index):
+        return start(remote(block(r, h), block(to, h), kv_s.at[0], kv_r.at[to, h], peer(dy=1)))
+
+    def minus(r, h):
         to = (r + 1) % NY
-        return start(remote(block(r, h), block(to, h), kv_s.at[index], kv_r.at[to, h], peer(dy=-1)))
+        return start(remote(block(r, h), block(to, h), kv_s.at[0], kv_r.at[to, h], peer(dy=-1)))
 
     def kv_arrived(r, h):
         remote(block(r, h), block(r, h), kv_s.at[0], kv_r.at[r, h], peer(dy=1)).wait_recv()
 
     def shared(r, h):
-        dst = kv.at[r, pl.ds(h * 2 * HALF + HALF, HALF)]
-        remote(dst, dst, sib_s.at[r, h], sib_r.at[r, h], peer(dc=1)).wait_recv()
+        dst = other(r, h)
+        remote(dst, dst, sib_s.at[0], sib_r.at[r, h], peer(dc=1)).wait_recv()
 
     half_rows = pl.ds(pl.multiple_of(core * 64, 64), 64)
 
     def w_right(hop):
         rows = half_rows if hop < 3 else pl.ds(pl.multiple_of(core * 64, 64), 32)
         src, to = (NZ - hop) % NZ, NZ - 1 - hop
-        start(remote(w_all.at[src, rows], w_all.at[to, rows], w_s.at[hop], w_r.at[to], peer(dz=1)))
+        start(remote(w_all.at[src, rows], w_all.at[to, rows], w_s.at[0], w_r.at[to], peer(dz=1)))
 
     def w_left(hop):
         rows = half_rows if hop < 3 else pl.ds(pl.multiple_of(core * 64 + 32, 32), 32)
         src, to = hop, hop + 1
         sem = w_r.at[to] if hop < 3 else w_r.at[0]
-        start(remote(w_all.at[src, rows], w_all.at[to, rows], w_s.at[4 + hop], sem, peer(dz=-1)))
+        start(remote(w_all.at[src, rows], w_all.at[to, rows], w_s.at[0], sem, peer(dz=-1)))
 
     def w_arrived(slot):
         if slot == 4:
@@ -150,12 +153,12 @@
             dst = w_all.at[slot, half_rows]
             remote(dst, dst, w_s.at[0], w_r.at[slot], peer(dz=1)).wait_recv()
         src = w_all.at[slot, half_rows]
-        start(remote(src, src, ws_s.at[slot], ws_r.at[slot], peer(dc=1)))
+        start(remote(src, src, ws_s.at[0], ws_r.at[slot], peer(dc=1)))
 
     def w_shared(slot):
         rows = pl.ds(pl.multiple_of((1 - core) * 64, 64), 64)
         dst = w_all.at[slot, rows]
-        remote(dst, dst, ws_s.at[slot], ws_r.at[slot], peer(dc=1)).wait_recv()
+        remote(dst, dst, ws_s.at[0], ws_r.at[slot], peer(dc=1)).wait_recv()
 
     def w_hop(hop):
         w_arrived(NZ - hop)
@@ -179,19 +182,26 @@
         weights = jnp.exp2(scores - new_top[:, 0:1])
         mixed = weights * tscores
         sum_w, sum_m = lane_sum(weights), lane_sum(mixed)
-        add = dot(weights.astype(BF16), kv[r, ks, 256:512])
-        add_m = dot(mixed.astype(BF16), kv[r, ks, 256:384])
-        add_t = add[:, 128:256] + add_m
+        weights, mixed = weights.astype(BF16), mixed.astype(BF16)
         if first:
             total[rs, :] = sum_w
             spread[rs, :] = sum_m
-            acc[rs, 0:128] = add[:, 0:128]
-            acc[rs, 128:256] = add_t
         else:
             total[rs, :] = total[rs, :] * factor + sum_w
             spread[rs, :] = spread[rs, :] * factor + sum_m
-            acc[rs, 0:128] = acc[rs, 0:128] * factor + add[:, 0:128]
-            acc[rs, 128:256] = acc[rs, 128:256] * factor + add_t
+        step = rows // 2
+        for i in (0, step):
+            add = dot(weights[i : i + step], kv[r, ks, 256:512])
+            add_m = dot(mixed[i : i + step], kv[r, ks, 256:384])
+            add_t = add[:, 128:256] + add_m
+            ps = pl.ds(lo + i, step)
+            if first:
+                acc[ps, 0:128] = add[:, 0:128]
+                acc[ps, 128:256] = add_t
+            else:
+                part = factor[i : i + step]
+                acc[ps, 0:128] = acc[ps, 0:128] * part + add[:, 0:128]
+                acc[ps, 128:256] = acc[ps, 128:256] * part + add_t
 
     def finish(lo):
         rs = pl.ds(lo, TOK)
@@ -205,54 +215,57 @@
     ld_k.wait()
     ld_v.wait()
     project_kv(0)
+    ld_w.wait()
     pl.semaphore_wait(barrier, len(friends))
-    plus(0, 0, 0)
+    plus(0, 0)
+    w_right(0)
+    w_left(0)
     share(0, 0)
     project_kv(1)
-    minus(0, 1, 3)
-    plus(0, 1, 1)
-    minus(0, 0, 4)
+    minus(0, 1)
+    plus(0, 1)
+    minus(0, 0)
     share(0, 1)
-    ld_w.wait()
-    w_right(0)
-    w_left(0)
     ld_q.wait()
-    qq[TOK : 2 * TOK, 128:256] = (dot(xt[0:TOK, :], wq[:, 256:384]) * (SCALE * LOG2E)).astype(BF16)
-    qq[TOK : 2 * TOK, 0:128] = (dot(xt[TOK : 2 * TOK, :], wq[:, 256:384]) * SCALE).astype(BF16)
+    for h in range(2):
+        rows = pl.ds(TOK + h * HALF, HALF)
+        flat = dot(xt[pl.ds(h * 2 * HALF, HALF), :], wq[:, 256:384])
+        tflat = dot(xt[pl.ds(h * 2 * HALF + HALF, HALF), :], wq[:, 256:384])
+        qq[rows, 128:256] = (flat * (SCALE * LOG2E)).astype(BF16)
+        qq[rows, 0:128] = (tflat * SCALE).astype(BF16)
     q_copy = start(remote(qq.at[pl.ds(TOK, TOK)], qq.at[pl.ds(0, TOK)], q_sem.at[0], q_sem.at[1], peer(dx=1)))
 
     shared(0, 0)
     shared(0, 1)
     attend(TOK, TOK, 0, 0, 1024, first=True)
     kv_arrived(3, 0)
-    plus(3, 0, 2)
+    plus(3, 0)
     share(3, 0)
     kv_arrived(1, 1)
-    minus(1, 1, 5)
+    minus(1, 1)
     share(1, 1)
+    w_hop(1)
     q_copy.wait_recv()
     attend(0, TOK, 0, 0, 1024, first=True)
-    w_hop(1)
     shared(3, 0)
     attend(0, 2 * TOK, 3, 0, 512)
-    shared(1, 1)
-    attend(0, 2 * TOK, 1, 512, 512)
     kv_arrived(3, 1)
     share(3, 1)
     kv_arrived(1, 0)
     share(1, 0)
+    shared(1, 1)
+    attend(0, 2 * TOK, 1, 512, 512)
     w_hop(2)
     shared(3, 1)
     attend(0, 2 * TOK, 3, 512, 512)
-    shared(1, 0)
-    attend(0, 2 * TOK, 1, 0, 512)
     kv_arrived(2, 0)
     share(2, 0)
     kv_arrived(2, 1)
     share(2, 1)
-    w_hop(3)
+    shared(1, 0)
+    attend(0, 2 * TOK, 1, 0, 512)
+    attend(0, 2 * TOK, 2, 0, 512)
     shared(2, 0)
-    attend(0, 2 * TOK, 2, 0, 512)
     shared(2, 1)
     attend(0, TOK, 2, 512, 512)
 
@@ -270,7 +283,8 @@
     part_copies = {}
     for k in ORDER:
         rows = piece(k)
-        part_copies[k] = start(remote(part_out.at[rows], part_in.at[rows], p_s.at[k], p_r.at[k], peer(dx=1)))
+        part_copies[k] = start(remote(part_out.at[rows], part_in.at[rows], p_s.at[0], p_r.at[k], peer(dx=1)))
+    w_hop(3)
     attend(TOK, TOK, 2, 512, 512)
     out, tangent, peak, weight, mean = finish(TOK)
     own_part[:, 0:128] = out
@@ -305,7 +319,7 @@
             a_out[k, PIECE : 2 * PIECE, :] = tmerged
             back = NZ - k
             dst = a_in.at[:, back * 128 : back * 128 + 128]
-            a_copies[k] = start(remote(a_out.at[k], dst, a_s.at[k], a_r.at[back], peer(dz=k)))
+            a_copies[k] = start(remote(a_out.at[k], dst, a_s.at[0], a_r.at[back], peer(dz=k)))
 
     w_arrived(4)
     for slot in range(1, NZ):
@@ -313,41 +327,54 @@
     for k in range(1, NZ):
         a_copies[k].wait_recv()
 
-    f_copies = {}
+    def columns(b, k):
+        column = (lax.rem(xh + b, NH) * NZ + lax.rem(z + k, NZ)) * 128
+        return w_all[:, :, pl.ds(pl.multiple_of(column, 128), 128)].reshape(NZ * 128, 128)
+
+    g_copies = {}
     for k in ORDER:
-        for b in (1, 0):
-            column = (lax.rem(xh + b, NH) * NZ + lax.rem(z + k, NZ)) * 128
-            rhs = w_all[:, :, pl.ds(pl.multiple_of(column, 128), 128)].reshape(NZ * 128, 128)
-            term = dot(a_in[...], rhs).astype(BF16)
-            if (b, k) == (0, 0):
-                f_in[0, 0] = term
-            else:
-                f_out[b, k] = term
-                back = (NZ - k) % NZ
-                f_copies[b, k] = start(
-                    remote(f_out.at[b, k], f_in.at[b, back], f_s.at[b, k], f_r.at[b, back], peer(dh=b, dz=k))
-                )
-    for k in range(NZ):
-        for b in range(NH):
-            if (b, k) != (0, 0):
-                remote(f_out.at[b, k], f_in.at[b, k], f_s.at[b, k], f_r.at[b, k], peer(dh=b, dz=k)).wait_recv()
-        rows = piece(k)
-        summed = f_in[0, k].astype(F32) + f_in[1, k].astype(F32)
-        out_ref[rows, :] = summed[0:PIECE].astype(BF16)
-        tout_ref[rows, :] = summed[PIECE : 2 * PIECE].astype(BF16)
-    for copy in sends:
-        copy.wait_send()
+        both = dot(a_in[...], jnp.concatenate([columns(1, k), columns(0, k)], axis=1))
+        g_out[k] = both[:, 0:128].astype(BF16)
+        g_copies[k] = start(remote(g_out.at[k], g_in.at[k], g_s.at[0], g_r.at[k], peer(dh=1)))
+        g_own[k] = both[:, 128:256]
+    for k in ORDER:
+        g_copies[k].wait_recv()
+        f_out[k] = (g_own[k] + g_in[k].astype(F32)).astype(BF16)
+        if k == 0:
+            mine = pltpu.make_async_copy(f_out.at[0], result.at[z], f_r.at[0])
+            mine.start()
+        else:
+            start(remote(f_out.at[k], result.at[z], f_s.at[0], f_r.at[NZ - k], peer(dz=k)))
+    sent(kv_s.at[0], xt.at[pl.ds(0, 6 * 64)])
+    sent(sib_s.at[0], xt.at[pl.ds(0, 8 * 64)])
+    sent(w_s.at[0], xt.at[pl.ds(0, 7 * 64)])
+    sent(ws_s.at[0], xt.at[pl.ds(0, 7 * 64)])
+    sent(p_s.at[0], part_out)
+    sent(a_s.at[0], a_out.at[pl.ds(1, NZ - 1)])
+    sent(g_s.at[0], g_out)
+    q_copy.wait_send()
+    stat_copy.wait_send()
+    mine.wait()
+    for k in range(1, NZ):
+        dst = result.at[lax.rem(z + k, NZ)]
+        remote(f_out.at[k], dst, f_s.at[0], f_r.at[k], peer(dz=k)).wait_recv()
+    sent(f_s.at[0], f_out.at[pl.ds(1, NZ - 1)])
+
+
+def split(result, out, tout):
+    out[...] = result[:, 0:PIECE, :]
+    tout[...] = result[:, PIECE : 2 * PIECE, :]
 
 
 def local(inputs, tangents, w_qkv, w_out):
     dma = pltpu.SemaphoreType.DMA
     vmem = pltpu.VMEM
-    return pl.pallas_call(
+    result = pl.pallas_call(
         kernel,
         name="tangent_attention",
-        out_shape=[jax.ShapeDtypeStruct((TOK, 128), BF16)] * 2,
+        out_shape=jax.ShapeDtypeStruct((NZ, 2 * PIECE, 128), BF16),
         in_specs=[pl.BlockSpec(memory_space=pl.ANY)] * 4,
-        out_specs=[pl.BlockSpec(memory_space=pltpu.VMEM)] * 2,
+        out_specs=pl.BlockSpec(memory_space=pl.ANY),
         scratch_shapes=[
             vmem((2 * TOK, D), BF16),
             vmem((D, 384), BF16),
@@ -366,30 +393,42 @@
             vmem((NZ, 128, 128), BF16),
             vmem((128, NZ * 128), BF16),
             vmem((NZ, 128, D), BF16),
-            vmem((NH, NZ, 128, 128), BF16),
-            vmem((NH, NZ, 128, 128), BF16),
-            dma((8,)),
-            dma((6,)),
+            vmem((NZ, 128, 128), BF16),
+            vmem((NZ, 128, 128), BF16),
+            vmem((NZ, 128, 128), F32),
+            vmem((NZ, 128, 128), BF16),
+            dma((8,)),
+            dma((1,)),
             dma((NY, 2)),
-            dma((NY, 2)),
+            dma((1,)),
             dma((NY, 2)),
             dma((2,)),
-            dma((8,)),
-            dma((8,)),
-            dma((8,)),
-            dma((8,)),
-            dma((8,)),
+            dma((1,)),
+            dma((8,)),
+            dma((1,)),
+            dma((8,)),
+            dma((1,)),
             dma((8,)),
             dma((2,)),
-            dma((8,)),
-            dma((8,)),
-            dma((NH, NZ)),
-            dma((NH, NZ)),
+            dma((1,)),
+            dma((8,)),
+            dma((1,)),
+            dma((8,)),
+            dma((1,)),
+            dma((8,)),
         ],
         compiler_params=pltpu.CompilerParams(
             collective_id=0, has_side_effects=True, vmem_limit_bytes=58 * 2**20
         ),
     )(inputs, tangents, w_qkv, w_out)
+    out, tout = pl.pallas_call(
+        split,
+        name="split",
+        out_shape=[jax.ShapeDtypeStruct((NZ, PIECE, 128), BF16)] * 2,
+        in_specs=[pl.BlockSpec(memory_space=pltpu.VMEM)],
+        out_specs=[pl.BlockSpec(memory_space=pltpu.VMEM)] * 2,
+    )(result)
+    return out.reshape(TOK, 128), tout.reshape(TOK, 128)
 
 
 def solution(mesh):

time: 65.8 us -> 57.3 us (0.87)
  Pallas kernels: 61.6 us -> 56.6 us
  local copies, waits for them, and re-layouts: 3.14 us -> 0 us
    pallas_call x1 -> x2, Pallas kernels: 61.6 us -> 56.6 us  [the longest x1 54.9 us: local(): pl.pallas_call(kernel, name='tangent_attention', out_shape=jax.ShapeDtype...]
    unnamed x2 -> x0, local copies, waits for them, and re-layouts: 3.14 us -> none
where the time goes in v2:
time: 57.3 us; the launch traced here: 57.2 us
  Pallas kernels  56.6 us (99%)
  between operations  0.64 us (1%)
    pallas_call x1, Pallas kernels, local(): pl.pallas_call(kernel, name='tangent_attention', out_shape=jax.ShapeDtype...  54.9 us
    pallas_call x1, Pallas kernels, local(): pl.pallas_call(split, name='split', out_shape=[jax.ShapeDtypeStruct((NZ,...  1.66 us

profile of v2, /device:TPU:8, one launch (start us, length us, event | category | flops | bytes accessed | tf_op | source)
XLA Modules:
  0.0 57.2 jit_solution(13322163044800857148)
XLA Ops:
  0.6 54.9 %tangent_attention.1.result = bf16[8,128,128]{2,1,0:T(8,128)(2,1)} custom-call(bf16[512,2048]{1,0:T(8,128)(2,1)} %x_hbm.1, bf16[512,2048]{1,0:T(8,128)(2,1)} %t_hbm.1, bf16[3,2048,128]{2,1,0:T(8,128)(2,1)} %wqkv_hbm.1, bf16[128,2048]{1,0:T(8,128)(2,1)} %wout_hbm.1), custom_call_target="tpu_custom_call" | custom-call | tf_op jit(solution)/shard_map/tangent_attention/pallas_call | solution.py:372
  55.6 1.7 %split.1 = (bf16[8,64,128]{2,1,0:T(8,128)(2,1)}, bf16[8,64,128]{2,1,0:T(8,128)(2,1)}) custom-call(bf16[8,128,128]{2,1,0:T(8,128)(2,1)} %tangent_attention.1.result), custom_call_target="tpu_custom_call" | custom-call | tf_op jit(solution)/shard_map/split/pallas_call | solution.py:424

commit v3 on v2

--- a/solution.py
+++ b/solution.py
@@ -38,13 +38,14 @@
 
 
 def kernel(
-    x_hbm, t_hbm, wqkv_hbm, wout_hbm, result,
+    x_hbm, t_hbm, wqkv_hbm, wout_hbm, both_ref,
     xt, wq, kv, qq, acc, top, total, spread,
     part_out, part_in, stat_out, stat_in, own_part, coef,
-    a_out, a_in, w_all, g_out, g_in, g_own, f_out,
+    a_out, a_in, w_all, g_out, g_in, g_own, f_out, f_in,
     ld, kv_s, kv_r, sib_s, sib_r, q_sem, w_s, w_r, ws_s, ws_r,
     p_s, p_r, st_sem, a_s, a_r, g_s, g_r, f_s, f_r,
 ):
+    out_ref, tout_ref = both_ref.at[pl.ds(0, TOK)], both_ref.at[pl.ds(TOK, TOK)]
     ctx = lax.axis_index("ctx")
     head = lax.axis_index("head")
     y, x, core = ctx // 4, (ctx // 2) % 2, ctx % 2
@@ -74,16 +75,14 @@
         copy.start()
         return copy
 
+    def load_rows(h):
+        rows = pl.ds(h * HALF, HALF)
+        first = load(x_hbm.at[rows], xt.at[pl.ds(2 * h * HALF, HALF)], 2 + h)
+        return first, load(t_hbm.at[rows], xt.at[pl.ds(2 * h * HALF + HALF, HALF)], 4 + h)
+
     ld_k = load(wqkv_hbm.at[1], wq.at[:, 0:128], 0)
     ld_v = load(wqkv_hbm.at[2], wq.at[:, 128:256], 1)
-    ld_x = [None, None]
-    ld_t = [None, None]
-    for h in range(2):
-        rows = pl.ds(h * HALF, HALF)
-        ld_x[h] = load(x_hbm.at[rows], xt.at[pl.ds(2 * h * HALF, HALF)], 2 + h)
-        ld_t[h] = load(t_hbm.at[rows], xt.at[pl.ds(2 * h * HALF + HALF, HALF)], 4 + h)
-    ld_w = load(wout_hbm, w_all.at[0], 7)
-    ld_q = load(wqkv_hbm.at[0], wq.at[:, 256:384], 6)
+    ld_rows = [load_rows(0)]
 
     def start(copy):
         copy.start()
@@ -94,8 +93,8 @@
 
     def project_kv(h):
         rows = pl.ds(h * 2 * HALF, HALF)
-        ld_x[h].wait()
-        ld_t[h].wait()
+        ld_rows[h][0].wait()
+        ld_rows[h][1].wait()
         flat = dot(xt[pl.ds(h * 2 * HALF, HALF), :], wq[:, 0:256])
         tflat = dot(xt[pl.ds(h * 2 * HALF + HALF, HALF), :], wq[:, 0:256])
         kv[0, rows, 0:128] = flat[:, 0:128].astype(BF16)
@@ -213,6 +212,9 @@
         return out, tangent, top[rs, 0:1], weight, mean
 
     ld_k.wait()
+    ld_rows.append(load_rows(1))
+    ld_w = load(wout_hbm, w_all.at[0], 7)
+    ld_q = load(wqkv_hbm.at[0], wq.at[:, 256:384], 6)
     ld_v.wait()
     project_kv(0)
     ld_w.wait()
@@ -258,23 +260,28 @@
     w_hop(2)
     shared(3, 1)
     attend(0, 2 * TOK, 3, 512, 512)
+    shared(1, 0)
+    attend(0, 2 * TOK, 1, 0, 512)
     kv_arrived(2, 0)
     share(2, 0)
     kv_arrived(2, 1)
     share(2, 1)
-    shared(1, 0)
-    attend(0, 2 * TOK, 1, 0, 512)
     attend(0, 2 * TOK, 2, 0, 512)
+    w_hop(3)
     shared(2, 0)
     shared(2, 1)
     attend(0, TOK, 2, 512, 512)
 
-    out, tangent, peak, weight, mean = finish(0)
+    lane = lax.broadcasted_iota(jnp.int32, (TOK, 128), 1)
+
+    def stat_rows(peak, weight, mean):
+        stats = jnp.where(lane == 0, peak, jnp.where(lane == 1, weight, mean))
+        return jnp.transpose(stats)[0:8, :]
+
+    out, tangent, *stats = finish(0)
     part_out[:, 0:128] = out.astype(BF16)
     part_out[:, 128:256] = tangent.astype(BF16)
-    lane = lax.broadcasted_iota(jnp.int32, (TOK, 128), 1)
-    stats = jnp.where(lane == 0, peak, jnp.where(lane == 1, weight, mean))
-    stat_out[...] = jnp.transpose(stats)[0:8, :]
+    stat_out[...] = stat_rows(*stats)
     stat_copy = start(remote(stat_out, stat_in, st_sem.at[0], st_sem.at[1], peer(dx=1)))
 
     def piece(k):
@@ -284,27 +291,29 @@
     for k in ORDER:
         rows = piece(k)
         part_copies[k] = start(remote(part_out.at[rows], part_in.at[rows], p_s.at[0], p_r.at[k], peer(dx=1)))
-    w_hop(3)
     attend(TOK, TOK, 2, 512, 512)
-    out, tangent, peak, weight, mean = finish(TOK)
+    out, tangent, *stats = finish(TOK)
     own_part[:, 0:128] = out
     own_part[:, 128:256] = tangent
+    own = stat_rows(*stats)
     stat_copy.wait_recv()
-    padded = jnp.concatenate([stat_in[...], jnp.zeros((120, TOK), F32)], axis=0)
-    other = jnp.transpose(padded)
-    peak2, weight2, mean2 = other[:, 0:1], other[:, 1:2], other[:, 2:3]
+    peak, weight, mean = own[0:1, :], own[1:2, :], own[2:3, :]
+    peak2, weight2, mean2 = stat_in[0:1, :], stat_in[1:2, :], stat_in[2:3, :]
     high = jnp.maximum(peak, peak2)
     mass = weight * jnp.exp2(peak - high)
     mass2 = weight2 * jnp.exp2(peak2 - high)
     inverse = 1.0 / (mass + mass2)
     p1, p2 = mass * inverse, mass2 * inverse
-    coef[0] = jnp.broadcast_to(p1, (TOK, 128))
-    coef[1] = jnp.broadcast_to(p2, (TOK, 128))
-    coef[2] = jnp.broadcast_to(p1 * p2 * (mean - mean2), (TOK, 128))
+    p3 = p1 * p2 * (mean - mean2)
+    columns = jnp.transpose(jnp.concatenate([p1, p2, p3, jnp.zeros((125, TOK), F32)], axis=0))
+    for i in range(3):
+        coef[i] = jnp.broadcast_to(columns[:, i : i + 1], (TOK, 128))
 
     a_copies = {}
     for k in ORDER:
         rows = piece(k)
+        if k == 6:
+            w_arrived(4)
         part_copies[k].wait_recv()
         o1, u1 = own_part[rows, 0:128], own_part[rows, 128:256]
         o2, u2 = part_in[rows, 0:128].astype(F32), part_in[rows, 128:256].astype(F32)
@@ -321,7 +330,6 @@
             dst = a_in.at[:, back * 128 : back * 128 + 128]
             a_copies[k] = start(remote(a_out.at[k], dst, a_s.at[0], a_r.at[back], peer(dz=k)))
 
-    w_arrived(4)
     for slot in range(1, NZ):
         w_shared(slot)
     for k in range(1, NZ):
@@ -339,12 +347,13 @@
         g_own[k] = both[:, 128:256]
     for k in ORDER:
         g_copies[k].wait_recv()
-        f_out[k] = (g_own[k] + g_in[k].astype(F32)).astype(BF16)
+        term = (g_own[k] + g_in[k].astype(F32)).astype(BF16)
         if k == 0:
-            mine = pltpu.make_async_copy(f_out.at[0], result.at[z], f_r.at[0])
-            mine.start()
+            out_ref[piece(0), :] = term[0:PIECE]
+            tout_ref[piece(0), :] = term[PIECE : 2 * PIECE]
         else:
-            start(remote(f_out.at[k], result.at[z], f_s.at[0], f_r.at[NZ - k], peer(dz=k)))
+            f_out[k] = term
+            start(remote(f_out.at[k], f_in.at[NZ - k], f_s.at[0], f_r.at[NZ - k], peer(dz=k)))
     sent(kv_s.at[0], xt.at[pl.ds(0, 6 * 64)])
     sent(sib_s.at[0], xt.at[pl.ds(0, 8 * 64)])
     sent(w_s.at[0], xt.at[pl.ds(0, 7 * 64)])
@@ -354,16 +363,12 @@
     sent(g_s.at[0], g_out)
     q_copy.wait_send()
     stat_copy.wait_send()
-    mine.wait()
-    for k in range(1, NZ):
-        dst = result.at[lax.rem(z + k, NZ)]
-        remote(f_out.at[k], dst, f_s.at[0], f_r.at[k], peer(dz=k)).wait_recv()
+    for k in ORDER:
+        if k != 0:
+            remote(f_in.at[k], f_in.at[k], f_s.at[0], f_r.at[k], peer(dz=k)).wait_recv()
+            out_ref[piece(k), :] = f_in[k, 0:PIECE]
+            tout_ref[piece(k), :] = f_in[k, PIECE : 2 * PIECE]
     sent(f_s.at[0], f_out.at[pl.ds(1, NZ - 1)])
-
-
-def split(result, out, tout):
-    out[...] = result[:, 0:PIECE, :]
-    tout[...] = result[:, PIECE : 2 * PIECE, :]
 
 
 def local(inputs, tangents, w_qkv, w_out):
@@ -372,9 +377,9 @@
     result = pl.pallas_call(
         kernel,
         name="tangent_attention",
-        out_shape=jax.ShapeDtypeStruct((NZ, 2 * PIECE, 128), BF16),
+        out_shape=pltpu.VMEM((2 * TOK, 128), BF16),
         in_specs=[pl.BlockSpec(memory_space=pl.ANY)] * 4,
-        out_specs=pl.BlockSpec(memory_space=pl.ANY),
+        out_specs=pl.BlockSpec(memory_space=pltpu.VMEM),
         scratch_shapes=[
             vmem((2 * TOK, D), BF16),
             vmem((D, 384), BF16),
@@ -397,6 +402,7 @@
             vmem((NZ, 128, 128), BF16),
             vmem((NZ, 128, 128), F32),
             vmem((NZ, 128, 128), BF16),
+            vmem((NZ, 128, 128), BF16),
             dma((8,)),
             dma((1,)),
             dma((NY, 2)),
@@ -421,14 +427,7 @@
             collective_id=0, has_side_effects=True, vmem_limit_bytes=58 * 2**20
         ),
     )(inputs, tangents, w_qkv, w_out)
-    out, tout = pl.pallas_call(
-        split,
-        name="split",
-        out_shape=[jax.ShapeDtypeStruct((NZ, PIECE, 128), BF16)] * 2,
-        in_specs=[pl.BlockSpec(memory_space=pltpu.VMEM)],
-        out_specs=[pl.BlockSpec(memory_space=pltpu.VMEM)] * 2,
-    )(result)
-    return out.reshape(TOK, 128), tout.reshape(TOK, 128)
+    return result[:TOK], result[TOK:]
 
 
 def solution(mesh):

time: 57.3 us -> 55.6 us (0.970)
  Pallas kernels: 56.6 us -> 54.2 us
  local copies, waits for them, and re-layouts: 0 us -> 0.72 us
    pallas_call x2 -> x1, Pallas kernels: 56.6 us -> 54.2 us  [local(): pl.pallas_call(kernel, name='tangent_attention', out_shape=pltpu.VMEM((2...]
    slice x0 -> x1, local copies, waits for them, and re-layouts: none -> 0.72 us  [local(): return (result[:TOK], result[TOK:])]
where the time goes in v3:
time: 55.6 us; the launch traced here: 55.5 us
  Pallas kernels  54.2 us (97%)
  local copies, waits for them, and re-layouts  0.72 us (1%)
  between operations  0.64 us (1%)
    pallas_call x1, Pallas kernels, local(): pl.pallas_call(kernel, name='tangent_attention', out_shape=pltpu.VMEM((2...  54.2 us

profile of v3, /device:TPU:8, one launch (start us, length us, event | category | flops | bytes accessed | tf_op | source)
XLA Modules:
  0.0 55.5 jit_solution(8847134092257682350)
XLA Ops:
  0.6 54.2 %tangent_attention.1 = bf16[1024,128]{1,0:T(8,128)(2,1)S(1)} custom-call(bf16[512,2048]{1,0:T(8,128)(2,1)} %x_hbm.1, bf16[512,2048]{1,0:T(8,128)(2,1)} %t_hbm.1, bf16[3,2048,128]{2,1,0:T(8,128)(2,1)} %wqkv_hbm.1, bf16[128,2048]{1,0:T(8,128)(2,1)} %wout_hbm.1), custom_call_target="tpu_custom_call" | custom-call | tf_op jit(solution)/shard_map/tangent_attention/pallas_call | solution.py:377
  54.8 0.7 %fusion = (bf16[512,128]{1,0:T(8,128)(2,1)}, bf16[512,128]{1,0:T(8,128)(2,1)}) fusion(bf16[1024,128]{1,0:T(8,128)(2,1)S(1)} %tangent_attention.1), kind=kLoop, calls=%fused_computation | loop fusion | bytes 524288 | tf_op jit(solution)/shard_map/slice | solution.py:430

commit v4 on v3

--- a/solution.py
+++ b/solution.py
@@ -21,7 +21,7 @@
 LOG2E = math.log2(math.e)
 LN2 = math.log(2.0)
 SCALE = HD ** (-0.5)
-ORDER = (4, 3, 5, 2, 6, 1, 7, 0)
+ORDER = (3, 5, 4, 2, 6, 1, 7, 0)
 
 
 def dot(a, b):

time: 55.6 us -> 55.2 us (level)
  no operation moved by 1% of the time
where the time goes in v4:
time: 55.2 us; the launch traced here: 55.1 us
  Pallas kernels  53.7 us (97%)
  local copies, waits for them, and re-layouts  0.72 us (1%)
  between operations  0.64 us (1%)
    pallas_call x1, Pallas kernels, local(): pl.pallas_call(kernel, name='tangent_attention', out_shape=pltpu.VMEM((2...  53.7 us

profile of v4, /device:TPU:8, one launch (start us, length us, event | category | flops | bytes accessed | tf_op | source)
XLA Modules:
  0.0 55.1 jit_solution(13715920171611574804)
XLA Ops:
  0.6 53.7 %tangent_attention.1 = bf16[1024,128]{1,0:T(8,128)(2,1)S(1)} custom-call(bf16[512,2048]{1,0:T(8,128)(2,1)} %x_hbm.1, bf16[512,2048]{1,0:T(8,128)(2,1)} %t_hbm.1, bf16[3,2048,128]{2,1,0:T(8,128)(2,1)} %wqkv_hbm.1, bf16[128,2048]{1,0:T(8,128)(2,1)} %wout_hbm.1), custom_call_target="tpu_custom_call" | custom-call | tf_op jit(solution)/shard_map/tangent_attention/pallas_call | solution.py:377
  54.4 0.7 %fusion = (bf16[512,128]{1,0:T(8,128)(2,1)}, bf16[512,128]{1,0:T(8,128)(2,1)}) fusion(bf16[1024,128]{1,0:T(8,128)(2,1)S(1)} %tangent_attention.1), kind=kLoop, calls=%fused_computation | loop fusion | bytes 524288 | tf_op jit(solution)/shard_map/slice | solution.py:430

commit v5 on v4

--- a/solution.py
+++ b/solution.py
@@ -312,7 +312,7 @@
     a_copies = {}
     for k in ORDER:
         rows = piece(k)
-        if k == 6:
+        if k == 1:
             w_arrived(4)
         part_copies[k].wait_recv()
         o1, u1 = own_part[rows, 0:128], own_part[rows, 128:256]

time: 55.2 us -> 55.2 us (level)
  no operation moved by 1% of the time
where the time goes in v5:
time: 55.2 us; the launch traced here: 55.1 us
  Pallas kernels  53.7 us (97%)
  local copies, waits for them, and re-layouts  0.72 us (1%)
  between operations  0.64 us (1%)
    pallas_call x1, Pallas kernels, local(): pl.pallas_call(kernel, name='tangent_attention', out_shape=pltpu.VMEM((2...  53.7 us

profile of v5, /device:TPU:8, one launch (start us, length us, event | category | flops | bytes accessed | tf_op | source)
XLA Modules:
  0.0 55.1 jit_solution(6973536581625336579)
XLA Ops:
  0.6 53.7 %tangent_attention.1 = bf16[1024,128]{1,0:T(8,128)(2,1)S(1)} custom-call(bf16[512,2048]{1,0:T(8,128)(2,1)} %x_hbm.1, bf16[512,2048]{1,0:T(8,128)(2,1)} %t_hbm.1, bf16[3,2048,128]{2,1,0:T(8,128)(2,1)} %wqkv_hbm.1, bf16[128,2048]{1,0:T(8,128)(2,1)} %wout_hbm.1), custom_call_target="tpu_custom_call" | custom-call | tf_op jit(solution)/shard_map/tangent_attention/pallas_call | solution.py:377
  54.4 0.7 %fusion = (bf16[512,128]{1,0:T(8,128)(2,1)}, bf16[512,128]{1,0:T(8,128)(2,1)}) fusion(bf16[1024,128]{1,0:T(8,128)(2,1)S(1)} %tangent_attention.1), kind=kLoop, calls=%fused_computation | loop fusion | bytes 524288 | tf_op jit(solution)/shard_map/slice | solution.py:430
